TPU v7x, 32 devices: a whole 2x2x4 slice. The times are simulated.
32 devices in a mesh: outer: 2 (over x), sec: 8 (over z, core), tp: 2 (over y).
Axes of the slice: x: 2, y: 2, z: 4, core: 2. Of those that a mesh axis runs over, the one named last changes fastest.
Arguments:
- tile_maps: bfloat16 [32, 12, 12, 3072], P(('outer', 'sec'), None, None, 'tp'), may hold values from -6 to 6
- tile_shape: int32 [32, 2], P(('outer', 'sec')), may hold values from 4 to 12
- conv_kernel: float32 [7, 7, 3072], P(None, None, 'tp'), may hold values from -0.875 to 0.875
- norm_gain: float32 [3072], P('tp'), may hold values from 0.25 to 1.75
- norm_bias: float32 [3072], P('tp'), may hold values from -3 to 3
- projector: bfloat16 [3072, 7168], P('tp', 'sec'), may hold values from -0.109375 to 0.109375
- text_rows: bfloat16 [9216, 7168], P(('outer', 'sec'), 'tp'), may hold values from -6 to 6
- row_order: int32 [16, 576], P(('outer', 'sec')), may hold values from 0 to 575, each once within a row
- seq_gain: float32 [7168], P('tp'), may hold values from 0.25 to 1.75
- cotangent: bfloat16 [9216, 7168], P(('outer', 'sec'), 'tp'), may hold values from -0.2772166 to 0.2772166, as said below
Outputs:
- normed: bfloat16 [9216, 7168], P(('outer', 'sec'), 'tp')
- kernel_delta: float32 [7, 7, 3072], P(None, None, 'tp')
- gain_delta: float32 [3072], P('tp')
- bias_delta: float32 [3072], P('tp')
Inputs may be any that keep to these rules, and one draw needn't show every extreme that they name: `row_order`: each row lists where the visual tokens arriving at that device stand, in arrival order, then the text rows. `tile_shape`: valid rows and columns of each tile, the rest of the map is padding. `cotangent`: gradient of the training loss.
All inputs are finite; a program needn't handle non-finite values.
Results may differ from a plain program's by a relative error of at most 0.0043.
Values may be sent and summed in bfloat16 or wider, within the bound.
A program may use at most 128 MiB of HBM per device.

v0:
```python
import jax
import jax.numpy as jnp
from jax import lax
from jax.sharding import PartitionSpec as P


def shape_mask(tile_shape, grid):
    places = lax.broadcasted_iota(jnp.int32, (1, grid), 1)
    rows_ok = places < tile_shape[:, 0:1]
    cols_ok = places < tile_shape[:, 1:2]
    return (rows_ok[:, :, None] & cols_ok[:, None, :]).astype(jnp.float32)


def on_device(
    tile_maps,
    tile_shape,
    conv_kernel,
    norm_gain,
    norm_bias,
    projector,
    text_rows,
    row_order,
    seq_gain,
    cotangent,
):
    grid = tile_maps.shape[1]
    half_ch = tile_maps.shape[3]
    channels = half_ch * lax.axis_size("tp")
    rows_dev = tile_maps.shape[0] * grid * grid
    width = text_rows.shape[1] * lax.axis_size("tp")
    validity = shape_mask(tile_shape, grid)[..., None]
    masked = tile_maps.astype(jnp.float32) * validity
    padded = jnp.pad(masked, ((0, 0), (3, 3), (3, 3), (0, 0)))
    conv_out = jnp.zeros(masked.shape, jnp.float32)
    for row_off in range(7):
        for col_off in range(7):
            conv_out = (
                conv_out
                + padded[:, row_off : row_off + grid, col_off : col_off + grid, :]
                * conv_kernel[row_off, col_off]
            )
    total_one, total_two = lax.psum(
        (jnp.sum(conv_out, axis=-1), jnp.sum(conv_out * conv_out, axis=-1)), "tp"
    )
    center = (total_one / channels)[..., None]
    inverse = lax.rsqrt((total_two / channels)[..., None] - center * center + 1e-06)
    normal = (conv_out - center) * inverse
    features = (
        (validity * (normal * norm_gain + norm_bias))
        .astype(jnp.bfloat16)
        .reshape(rows_dev, half_ch)
    )
    tp_size = lax.axis_size("tp")
    half_width = text_rows.shape[1]
    mine = lax.axis_index("tp")
    swap = [(i, (i + 1) % tp_size) for i in range(tp_size)]
    gathered = lax.all_gather(projector, "sec", axis=0, tiled=False)
    per_half = gathered.shape[0] // tp_size
    own_weight = lax.dynamic_slice_in_dim(gathered, mine * per_half, per_half, axis=0)
    far_weight = lax.dynamic_slice_in_dim(gathered, (1 - mine) * per_half, per_half, axis=0)
    routed = lax.all_to_all(features, "sec", split_axis=0, concat_axis=0, tiled=True)

    def project(rows, weight):
        return jnp.concatenate(
            [
                jnp.dot(rows, weight[block], preferred_element_type=jnp.float32)
                for block in range(per_half)
            ],
            axis=1,
        )

    sent = project(routed, far_weight).astype(jnp.bfloat16)
    other = lax.ppermute(sent, "tp", swap)
    arrived = (project(routed, own_weight) + other.astype(jnp.float32)).astype(jnp.bfloat16)
    positions = row_order[0, :rows_dev]
    merged = text_rows.at[positions].set(arrived)
    wide = merged.astype(jnp.float32)
    upstream = cotangent.astype(jnp.float32) * seq_gain
    square_sum, along = lax.psum(
        (jnp.sum(wide * wide, axis=-1), jnp.sum(upstream * wide, axis=-1)), "tp"
    )
    inv_rms = lax.rsqrt(square_sum / width + 1e-05)[:, None]
    normed = (wide * inv_rms * seq_gain).astype(jnp.bfloat16)
    grad_seq = inv_rms * upstream - wide * (inv_rms * inv_rms * inv_rms) * along[:, None] / width
    picked = grad_seq[positions].astype(jnp.bfloat16)
    far_picked = lax.ppermute(picked, "tp", swap)

    def project_back(rows, weight):
        step = weight.shape[2]
        total = jnp.zeros((rows.shape[0], half_ch), jnp.float32)
        for block in range(per_half):
            total = total + lax.dot_general(
                rows[:, block * step : (block + 1) * step],
                weight[block],
                (((1,), (1,)), ((), ())),
                preferred_element_type=jnp.float32,
            )
        return total

    back = (project_back(picked, own_weight) + project_back(far_picked, far_weight)).astype(
        jnp.bfloat16
    )
    grad_rows = lax.all_to_all(back, "sec", split_axis=0, concat_axis=0, tiled=True).astype(
        jnp.float32
    )
    masked_grad = grad_rows.reshape(masked.shape) * validity
    scaled = masked_grad * norm_gain
    first_sum, second_sum = lax.psum(
        (jnp.sum(scaled, axis=-1), jnp.sum(scaled * normal, axis=-1)), "tp"
    )
    grad_conv = inverse * (
        scaled - (first_sum / channels)[..., None] - normal * (second_sum / channels)[..., None]
    )
    kernel_rows = []
    for row_off in range(7):
        for col_off in range(7):
            window = padded[:, row_off : row_off + grid, col_off : col_off + grid, :]
            kernel_rows.append(jnp.sum(window * grad_conv, axis=(0, 1, 2)))
    gain_grad = jnp.sum(masked_grad * normal, axis=(0, 1, 2))
    bias_grad = jnp.sum(masked_grad, axis=(0, 1, 2))
    local_delta = jnp.stack(kernel_rows + [gain_grad, bias_grad], axis=0)
    pods = lax.axis_size("outer")
    entries = 51 * channels
    pod_sum = lax.psum(local_delta, "sec")
    norm_sq = lax.psum(jnp.sum(pod_sum * pod_sum), "tp")
    factor = jnp.minimum(1.0, 1.0 / jnp.sqrt(norm_sq / entries + 1e-06))
    average = lax.psum(pod_sum * factor, "outer") / pods
    return (normed, average[:49].reshape(7, 7, half_ch), average[49], average[50])


def solution(mesh):
    in_specs = (
        P(("outer", "sec"), None, None, "tp"),
        P(("outer", "sec"), None),
        P(None, None, "tp"),
        P("tp"),
        P("tp"),
        P("tp", "sec"),
        P(("outer", "sec"), "tp"),
        P(("outer", "sec"), None),
        P("tp"),
        P(("outer", "sec"), "tp"),
    )
    out_specs = (P(("outer", "sec"), "tp"), P(None, None, "tp"), P("tp"), P("tp"))
    return jax.shard_map(
        on_device, mesh=mesh, in_specs=in_specs, out_specs=out_specs, check_vma=False
    )
```

profile of v0, /device:TPU:0, one launch (start us, length us, event | category | flops | bytes accessed | tf_op | source)
XLA Modules:
  0.0 554.4 jit_solution(14218790435124544517)
XLA Ops:
  7.2 4.4 copy.22
  14.4 23.6 %fusion.53 = (f32[2,12,12]{2,1,0:T(8,128)S(1)}, f32[2,12,12]{2,1,0:T(8,128)S(1)}, f32[2,12,12,1536]{3,2,1,0:T(8,128)}) fusion(f32[1536]{0:T(1024)S(1)} %get-tuple-element.110, f32[1536]{0:T(1024)S(1)} %get-tuple-element.111, f32[1536]{0:T(1024)S(1)} %get-tuple-element.64, f32[1536]{0:T(1024)S(1)} %get-tuple-element.65, f32[1536]{0:T(1024)S(1)} %get-tuple-element.66, ...), kind=kLoop, calls=%fused_computation.248 | loop fusion | flops 44236224 | bytes 3842304 | tf_op jit(solution)/shard_map/reduce_sum | solution.py:43
  38.1 9.8 %all-reduce.3 = (f32[2,12,12]{2,1,0:T(8,128)S(1)}, f32[2,12,12]{2,1,0:T(8,128)S(1)}) all-reduce(f32[2,12,12]{2,1,0:T(8,128)S(1)} %get-tuple-element.58, f32[2,12,12]{2,1,0:T(8,128)S(1)} %get-tuple-element.57), channel_id=1, replica_groups=mesh['outer'=2,'sec'=8,'tp'=2] {'tp'}, use_global_device_ids=true, to_apply=%region_3.4 | all-reduce | flops 576 | bytes 4608 | tf_op jit(solution)/shard_map/psum | solution.py:42
  48.6 3.4 multiply_convert_fusion
  53.1 5.4 all-to-all-start
  58.5 54.2 %all-to-all-done = bf16[8,36,1536]{2,1,0:T(8,128)(2,1)S(1)} async-done(((bf16[8,36,1536]{2,1,0:T(8,128)(2,1)}), bf16[8,36,1536]{2,1,0:T(8,128)(2,1)S(1)}, u32[]{:S(2)}, u32[]{:S(2)}) %all-to-all-start) | async-done | bytes 884768 | tf_op jit(solution)/shard_map/all_to_all | solution.py:61
  113.8 115.7 %all-gather.3.cloned.1.call-done = bf16[12288,896]{1,0:T(8,128)(2,1)} async-done(((bf16[1536,896]{1,0:T(8,128)(2,1)}), bf16[12288,896]{1,0:T(8,128)(2,1)}) %all-gather.3.cloned.1.call-update) | async-done | bytes 22020112 | tf_op jit(solution)/shard_map/all_gather | solution.py:57
  229.5 3.2 fusion.27
  255.8 34.5 %collective-permute-done = bf16[288,3584]{1,0:T(8,128)(2,1)} collective-permute-done((bf16[288,3584]{1,0:T(8,128)(2,1)}, bf16[288,3584]{1,0:T(8,128)(2,1)}, u32[]{:S(2)}, u32[]{:S(2)}) %collective-permute-start) | collective-permute-done | bytes 2064416 | tf_op jit(solution)/shard_map/ppermute | solution.py:73
  290.3 3.4 fusion.7
  293.7 9.2 %scatter_fusion = bf16[576,3584]{1,0:T(8,128)(2,1)} fusion(bf16[576,3584]{1,0:T(8,128)(2,1)} %copy.22, s32[288]{0:T(512)S(1)} %fusion.52, bf16[288,3584]{1,0:T(8,128)(2,1)} %fusion.7), kind=kCustom, calls=%fused_computation.1 | custom fusion | bytes 6194304 | tf_op jit(solution)/shard_map/scatter | solution.py:76
  302.9 5.4 fusion.6
  308.3 5.2 all-reduce.2
  313.5 6.7 %fusion.5 = bf16[576,3584]{1,0:T(8,128)(2,1)} fusion(bf16[576,3584]{1,0:T(8,128)(2,1)} %scatter_fusion, bf16[576,3584]{1,0:T(8,128)(2,1)} %param.19, f32[576]{0:T(1024)S(1)} %get-tuple-element.117, f32[576]{0:T(1024)S(1)} %get-tuple-element.124, f32[3584]{0:T(1024)S(1)} %copy-done.9, f32[576]{0:T(1024)S(1)} %get-tuple-element.125), kind=kLoop, calls=%fused_computation.59 | loop fusion | flops 18579456 | bytes 12407552 | tf_op jit(solution)/shard_map/sub | solution.py:84
  320.2 10.0 %gather_fusion = bf16[288,3584]{1,0:T(8,128)(2,1)} fusion(bf16[576,3584]{1,0:T(8,128)(2,1)} %fusion.5, s32[1024]{0:T(1024)S(1)} %pad_clamp_fusion), kind=kCustom, calls=%fused_computation | custom fusion | bytes 4129920 | tf_op jit(solution)/shard_map/gather | solution.py:85
  331.7 3.0 fusion.12
  334.8 2.9 convolution_add_fusion.3
  340.6 2.9 convolution_add_fusion.1
  343.6 32.0 %collective-permute-done.1 = bf16[288,3584]{1,0:T(8,128)(2,1)S(1)} collective-permute-done((bf16[288,3584]{1,0:T(8,128)(2,1)}, bf16[288,3584]{1,0:T(8,128)(2,1)S(1)}, u32[]{:S(2)}, u32[]{:S(2)}) %collective-permute-start.1) | collective-permute-done | bytes 2064416 | tf_op jit(solution)/shard_map/ppermute | solution.py:86
  384.3 3.0 fusion.11
  388.4 3.9 all-to-all-start.1
  392.4 25.0 %all-to-all-done.1 = bf16[8,36,1536]{2,1,0:T(8,128)(2,1)S(1)} async-done(((bf16[8,36,1536]{2,1,0:T(8,128)(2,1)}), bf16[8,36,1536]{2,1,0:T(8,128)(2,1)S(1)}, u32[]{:S(2)}, u32[]{:S(2)}) %all-to-all-start.1) | async-done | bytes 884768 | tf_op jit(solution)/shard_map/all_to_all | solution.py:103
  418.9 3.4 multiply_reduce_fusion
  422.9 8.5 %all-reduce.1 = (f32[2,12,12]{2,1,0:T(8,128)S(1)}, f32[2,12,12]{2,1,0:T(8,128)S(1)}) all-reduce(f32[2,12,12]{2,1,0:T(8,128)S(1)} %get-tuple-element.5, f32[2,12,12]{2,1,0:T(8,128)S(1)} %reduce_sum.529), channel_id=1, replica_groups=mesh['outer'=2,'sec'=8,'tp'=2] {'tp'}, use_global_device_ids=true, to_apply=%region_12.13 | all-reduce | flops 576 | bytes 4608 | tf_op jit(solution)/shard_map/psum | solution.py:108
  431.4 9.6 %multiply_reduce_fusion.1 = (f32[1536]{0:T(1024)S(1)}, f32[1536]{0:T(1024)S(1)}, f32[1536]{0:T(1024)S(1)}, f32[1536]{0:T(1024)S(1)}, f32[1536]{0:T(1024)S(1)}, /...) fusion(f32[2,12,12,1536]{3,2,1,0:T(8,128)S(1)} %convert_multipl, ...), kind=kLoop, calls=%fused_computation.93 | loop fusion | flops 19436544 | bytes 7200384 | tf_op jit(solution)/shard_map/reduce_sum | solution.py:118
  441.0 5.4 multiply_reduce_fusion.38
  446.4 6.3 %multiply_reduce_fusion.19 = (f32[1536]{0:T(1024)S(1)}, f32[1536]{0:T(1024)S(1)}, f32[1536]{0:T(1024)S(1)}, f32[1536]{0:T(1024)S(1)}, f32[1536]{0:T(1024)S(1)}, ...) fusion(f32[2,12,12,1536]{3,2,1,0:T(8,128)S(1)} %get-tuple-eleme, ...), kind=kLoop, calls=%fused_computation.111 | loop fusion | flops 15897600 | bytes 3649536 | tf_op jit(solution)/shard_map/reduce_sum | solution.py:118
  453.5 4.8 stack.207
  458.4 51.0 %all-reduce.7.cloned.1.call-done = f32[51,1536]{1,0:T(8,128)} async-done(((f32[51,1536]{1,0:T(8,128)}), f32[51,1536]{1,0:T(8,128)}) %all-reduce.7.cloned.1.call-update) | async-done | bytes 313360 | tf_op jit(solution)/shard_map/psum | solution.py:124
  511.0 5.5 %psum.70 = f32[]{:T(128)} all-reduce(f32[]{:T(128)} %multiply_reduce_fusion.54), channel_id=1, replica_groups=mesh['outer'=2,'sec'=8,'tp'=2] {'tp'}, use_global_device_ids=true, to_apply=%region_66.67 | all-reduce | flops 1 | bytes 8 | tf_op jit(solution)/shard_map/psum | solution.py:125
  519.0 5.5 fusion.2
  524.6 20.6 %all-reduce.9.cloned.1.call-done = f32[51,1536]{1,0:T(8,128)} async-done(((f32[51,1536]{1,0:T(8,128)}), f32[51,1536]{1,0:T(8,128)}) %all-reduce.9.cloned.1.call-update) | async-done | bytes 313360 | tf_op jit(solution)/shard_map/psum | solution.py:127
  (122 shorter events, 51.2 us)
Async XLA Ops:
  7.2 222.4 %all-gather.3.cloned.1.call-start = ((), (), s32[]{:S(2)}) async-start(), calls=%async_computation.4 | async-start | bytes 24772608 | tf_op jit(solution)/shard_map/all_gather | solution.py:57
  11.6 0.7 copy-start.11
  11.6 1.0 copy-start.4
  11.6 2.6 copy-start.1
  47.9 0.6 copy-start.5
  47.9 0.6 copy-start.7
  53.1 59.6 %all-to-all-start = ((bf16[8,36,1536]{2,1,0:T(8,128)(2,1)}), bf16[8,36,1536]{2,1,0:T(8,128)(2,1)S(1)}, u32[]{:S(2)}, u32[]{:S(2)}) async-start(bf16[8,36,1536]{2,1,0:T(8,128)(2,1)} %all_to_all.14), calls=%async_computation | async-start | bytes 1966080 | tf_op jit(solution)/shard_map/all_to_all | solution.py:61
  229.5 3.2 copy-start.3
  241.4 3.0 copy-start.12
  242.9 47.4 %collective-permute-start = (bf16[288,3584]{1,0:T(8,128)(2,1)}, bf16[288,3584]{1,0:T(8,128)(2,1)}, u32[]{:S(2)}, u32[]{:S(2)}) collective-permute-start(bf16[288,3584]{1,0:T(8,128)(2,1)} %pad_maximum_fusion), channel_id=1, source_target_pairs={{0,1},{1,0},{2,3},{3,2},{4,5},{5,4},{6,7},{7,6},{8,9},{9,8},{10,11... | collective-permute-start | bytes 6193160 | tf_op jit(solution)/shard_map/ppermute | solution.py:73
  293.7 9.2 %copy-start.9 = (f32[3584]{0:T(1024)S(1)}, f32[3584]{0:T(1024)}, u32[]{:S(2)}) copy-start(f32[3584]{0:T(1024)} %param.18) | copy-start | bytes 43012
  330.3 4.5 copy-start
  330.3 45.3 %collective-permute-start.1 = (bf16[288,3584]{1,0:T(8,128)(2,1)}, bf16[288,3584]{1,0:T(8,128)(2,1)S(1)}, u32[]{:S(2)}, u32[]{:S(2)}) collective-permute-start(bf16[288,3584]{1,0:T(8,128)(2,1)} %gather_fusion), channel_id=1, source_target_pairs={{0,1},{1,0},{2,3},{3,2},{4,5},{5,4},{6,7},{7,6},{8,9},{9,8},{10,11... | collective-permute-start | bytes 6193160 | tf_op jit(solution)/shard_map/ppermute | solution.py:86
  388.4 30.5 %copy-start.6 = (f32[2,12,12]{2,1,0:T(8,128)S(1)}, f32[2,12,12]{2,1,0:T(8,128)}, u32[]{:S(2)}) copy-start(f32[2,12,12]{2,1,0:T(8,128)} %copy-done.5) | copy-start | bytes 3460
  388.4 30.5 %copy-start.8 = (f32[2,12,12]{2,1,0:T(8,128)S(1)}, f32[2,12,12]{2,1,0:T(8,128)}, u32[]{:S(2)}) copy-start(f32[2,12,12]{2,1,0:T(8,128)} %copy-done.7) | copy-start | bytes 3460
  388.4 30.5 %copy-start.10 = (f32[1536]{0:T(1024)S(1)}, f32[1536]{0:T(1024)}, u32[]{:S(2)}) copy-start(f32[1536]{0:T(1024)} %param.13) | copy-start | bytes 18436
  388.4 29.0 %all-to-all-start.1 = ((bf16[8,36,1536]{2,1,0:T(8,128)(2,1)}), bf16[8,36,1536]{2,1,0:T(8,128)(2,1)S(1)}, u32[]{:S(2)}, u32[]{:S(2)}) async-start(bf16[8,36,1536]{2,1,0:T(8,128)(2,1)} %all_to_all.17), calls=%async_computation.1 | async-start | bytes 1966080 | tf_op jit(solution)/shard_map/all_to_all | solution.py:103
  392.3 117.0 %all-reduce.7.cloned.1.call-start = ((), (), s32[]{:S(2)}) async-start(), calls=%async_computation.2 | async-start | bytes 688128 | tf_op jit(solution)/shard_map/psum | solution.py:124
  431.3 9.6 %copy-start.2 = (bf16[2,12,12,1536]{3,0,2,1:T(2,128)(2,1)S(1)}, bf16[2,12,12,1536]{3,0,2,1:T(2,128)(2,1)}, u32[]{:S(2)}) copy-start(bf16[2,12,12,1536]{3,0,2,1:T(2,128)(2,1)} %param.10) | copy-start | bytes 2654212
  458.3 86.9 %all-reduce.9.cloned.1.call-start = ((), (), s32[]{:S(2)}) async-start(), calls=%async_computation.3 | async-start | bytes 688128 | tf_op jit(solution)/shard_map/psum | solution.py:127
Sparse Core Ops, SparseCore 0:
  11.8 217.7 all-gather.2
  458.4 50.8 all-reduce.6
  519.2 25.9 all-reduce.8
where the time goes:
time: 561 us; the launch traced here: 554 us
  waiting for transfers between devices  333 us (59%)
  other arithmetic  79.7 us (14%)
  matrix products  46.6 us (8%)
  local copies, waits for them, and re-layouts  38.2 us (7%)
  blocking collectives  29 us (5%)
  between operations  15.4 us (3%)
  starting transfers between devices  12.3 us (2%)
    all_gather x1, waiting for transfers between devices, on_device(): gathered = lax.all_gather(projector, 'sec', axis=0, tiled=False)  116 us
    all_to_all x1, waiting for transfers between devices, on_device(): lax.all_to_all(features, 'sec', split_axis=0, concat_axis=0, tiled=True)  54.2 us
    psum x1, waiting for transfers between devices, on_device(): pod_sum = lax.psum(local_delta, 'sec')  51 us
    ppermute x1, waiting for transfers between devices, on_device(): other = lax.ppermute(sent, 'tp', swap)  34.5 us
    ppermute x1, waiting for transfers between devices, on_device(): far_picked = lax.ppermute(picked, 'tp', swap)  32 us
    all_to_all x1, waiting for transfers between devices, on_device(): lax.all_to_all(back, 'sec', split_axis=0, concat_axis=0, tiled=True)  25 us
    reduce_sum x1, other arithmetic, on_device(): jnp.sum(conv_out, axis=-1)  23.6 us
    dot_general x8, matrix products, project_back(): lax.dot_general(rows[:, block * step:(block + 1) * step], weight[block],...  23.4 us
  transfers between devices with their start and end apart: 7, of which 7 were waited for; matrix products, arithmetic and copies ran while one was open for 10% of the time, Pallas kernels for 0%

commit v1 on v0

--- a/solution.py
+++ b/solution.py
@@ -2,6 +2,18 @@
 import jax.numpy as jnp
 from jax import lax
 from jax.sharding import PartitionSpec as P
+
+
+def sent_to_each(x, axis, split, join):
+    ways, here = (lax.axis_size(axis), lax.axis_index(axis))
+    width = x.shape[split] // ways
+    turned = jnp.roll(x, -here * width, axis=split)
+    got = [lax.slice_in_dim(turned, 0, width, axis=split)]
+    for far in range(1, ways):
+        sent = lax.slice_in_dim(turned, far * width, (far + 1) * width, axis=split)
+        got.append(lax.ppermute(sent, axis, [(d, (d + far) % ways) for d in range(ways)]))
+    line = jnp.concatenate(got[::-1], axis=join)
+    return jnp.roll(line, (here + 1) * got[0].shape[join], axis=join)
 
 
 def shape_mask(tile_shape, grid):
@@ -100,9 +112,7 @@
     back = (project_back(picked, own_weight) + project_back(far_picked, far_weight)).astype(
         jnp.bfloat16
     )
-    grad_rows = lax.all_to_all(back, "sec", split_axis=0, concat_axis=0, tiled=True).astype(
-        jnp.float32
-    )
+    grad_rows = sent_to_each(back, "sec", 0, 0).astype(jnp.float32)
     masked_grad = grad_rows.reshape(masked.shape) * validity
     scaled = masked_grad * norm_gain
     first_sum, second_sum = lax.psum(

time: 561 us -> 568 us (1.012)
  local copies, waits for them, and re-layouts: 38.2 us -> 47.2 us
  waiting for transfers between devices: 333 us -> 327 us
    all_to_all x1 -> x0, waiting for transfers between devices: 25 us -> none  [on_device(): lax.all_to_all(back, 'sec', split_axis=0, concat_axis=0, tiled=True)]
    ppermute x0 -> x7, waiting for transfers between devices: none -> 13.2 us  [sent_to_each(): lax.ppermute(sent, axis, [(d, (d + far) % ways) for d in range(ways)])]
    concatenate x0 -> x1, local copies, waits for them, and re-layouts: none -> 6.06 us  [sent_to_each(): line = jnp.concatenate(got[::-1], axis=join)]
  transfers between devices with their start and end apart: 7 -> 13, of which waited for: 7 -> 10; matrix products, arithmetic and copies ran while one was open for 10% -> 10% of each run, Pallas kernels for 0% -> 0%
where the time goes in v1:
time: 568 us; the launch traced here: 562 us
  waiting for transfers between devices  327 us (58%)
  other arithmetic  82.5 us (15%)
  matrix products  47.5 us (8%)
  local copies, waits for them, and re-layouts  47.2 us (8%)
  blocking collectives  28.7 us (5%)
  between operations  15.5 us (3%)
  starting transfers between devices  13 us (2%)
    all_gather x1, waiting for transfers between devices, on_device(): gathered = lax.all_gather(projector, 'sec', axis=0, tiled=False)  116 us
    psum x1, waiting for transfers between devices, on_device(): pod_sum = lax.psum(local_delta, 'sec')  56.6 us
    all_to_all x1, waiting for transfers between devices, on_device(): lax.all_to_all(features, 'sec', split_axis=0, concat_axis=0, tiled=True)  54.4 us
    ppermute x1, waiting for transfers between devices, on_device(): other = lax.ppermute(sent, 'tp', swap)  34.5 us
    ppermute x1, waiting for transfers between devices, on_device(): far_picked = lax.ppermute(picked, 'tp', swap)  32 us
    dot_general x8, matrix products, project_back(): lax.dot_general(rows[:, block * step:(block + 1) * step], weight[block],...  24.3 us
    reduce_sum x1, other arithmetic, on_device(): jnp.sum(conv_out, axis=-1)  23.6 us
    dot_general x8, matrix products, project(): jnp.dot(rows, weight[block], preferred_element_type=jnp.float32)  23.2 us
  transfers between devices with their start and end apart: 13, of which 10 were waited for; matrix products, arithmetic and copies ran while one was open for 10% of the time, Pallas kernels for 0%

profile of v1, /device:TPU:0, one launch (start us, length us, event | category | flops | bytes accessed | tf_op | source)
XLA Modules:
  0.0 561.5 jit_solution(13421777247876512216)
XLA Ops:
  7.2 4.4 copy.23
  14.4 23.6 %fusion.56 = (f32[2,12,12]{2,1,0:T(8,128)S(1)}, f32[2,12,12]{2,1,0:T(8,128)S(1)}, f32[2,12,12,1536]{3,2,1,0:T(8,128)}) fusion(f32[1536]{0:T(1024)S(1)} %get-tuple-element.111, f32[1536]{0:T(1024)S(1)} %get-tuple-element.112, f32[1536]{0:T(1024)S(1)} %get-tuple-element.65, f32[1536]{0:T(1024)S(1)} %get-tuple-element.66, f32[1536]{0:T(1024)S(1)} %get-tuple-element.67, ...), kind=kLoop, calls=%fused_computation.255 | loop fusion | flops 44236224 | bytes 3842304 | tf_op jit(solution)/shard_map/reduce_sum | solution.py:55
  38.1 9.8 %all-reduce.3 = (f32[2,12,12]{2,1,0:T(8,128)S(1)}, f32[2,12,12]{2,1,0:T(8,128)S(1)}) all-reduce(f32[2,12,12]{2,1,0:T(8,128)S(1)} %get-tuple-element.59, f32[2,12,12]{2,1,0:T(8,128)S(1)} %get-tuple-element.58), channel_id=1, replica_groups=mesh['outer'=2,'sec'=8,'tp'=2] {'tp'}, use_global_device_ids=true, to_apply=%region_3.4 | all-reduce | flops 576 | bytes 4608 | tf_op jit(solution)/shard_map/psum | solution.py:54
  48.6 3.4 multiply_convert_fusion
  53.1 4.9 all-to-all-start
  58.3 54.4 %all-to-all-done = bf16[8,36,1536]{2,1,0:T(8,128)(2,1)S(1)} async-done(((bf16[8,36,1536]{2,1,0:T(8,128)(2,1)}), bf16[8,36,1536]{2,1,0:T(8,128)(2,1)S(1)}, u32[]{:S(2)}, u32[]{:S(2)}) %all-to-all-start) | async-done | bytes 884768 | tf_op jit(solution)/shard_map/all_to_all | solution.py:73
  113.8 115.7 %all-gather.3.cloned.1.call-done = bf16[12288,896]{1,0:T(8,128)(2,1)} async-done(((bf16[1536,896]{1,0:T(8,128)(2,1)}), bf16[12288,896]{1,0:T(8,128)(2,1)}) %all-gather.3.cloned.1.call-update) | async-done | bytes 22020112 | tf_op jit(solution)/shard_map/all_gather | solution.py:69
  229.5 3.2 fusion.27
  255.8 34.5 %collective-permute-done = bf16[288,3584]{1,0:T(8,128)(2,1)} collective-permute-done((bf16[288,3584]{1,0:T(8,128)(2,1)}, bf16[288,3584]{1,0:T(8,128)(2,1)}, u32[]{:S(2)}, u32[]{:S(2)}) %collective-permute-start) | collective-permute-done | bytes 2064416 | tf_op jit(solution)/shard_map/ppermute | solution.py:85
  290.3 3.4 fusion.7
  293.7 9.7 %scatter_fusion = bf16[576,3584]{1,0:T(8,128)(2,1)} fusion(bf16[576,3584]{1,0:T(8,128)(2,1)} %copy.23, s32[288]{0:T(512)S(1)} %fusion.55, bf16[288,3584]{1,0:T(8,128)(2,1)} %fusion.7), kind=kCustom, calls=%fused_computation.1 | custom fusion | bytes 6194304 | tf_op jit(solution)/shard_map/scatter | solution.py:88
  303.4 5.4 fusion.6
  308.9 5.0 all-reduce.2
  313.9 6.7 %fusion.5 = bf16[576,3584]{1,0:T(8,128)(2,1)} fusion(bf16[576,3584]{1,0:T(8,128)(2,1)} %scatter_fusion, bf16[576,3584]{1,0:T(8,128)(2,1)} %param.21, f32[576]{0:T(1024)S(1)} %get-tuple-element.118, f32[576]{0:T(1024)S(1)} %get-tuple-element.134, f32[3584]{0:T(1024)S(1)} %copy-done.9, f32[576]{0:T(1024)S(1)} %get-tuple-element.135), kind=kLoop, calls=%fused_computation.59 | loop fusion | flops 18579456 | bytes 12407552 | tf_op jit(solution)/shard_map/sub | solution.py:96
  320.6 10.2 %gather_fusion = bf16[288,3584]{1,0:T(8,128)(2,1)} fusion(bf16[576,3584]{1,0:T(8,128)(2,1)} %fusion.5, s32[1024]{0:T(1024)S(1)} %pad_clamp_fusion), kind=kCustom, calls=%fused_computation | custom fusion | bytes 4129920 | tf_op jit(solution)/shard_map/gather | solution.py:97
  332.4 3.2 fusion.12
  344.3 32.0 %collective-permute-done.1 = bf16[288,3584]{1,0:T(8,128)(2,1)} collective-permute-done((bf16[288,3584]{1,0:T(8,128)(2,1)}, bf16[288,3584]{1,0:T(8,128)(2,1)}, u32[]{:S(2)}, u32[]{:S(2)}) %collective-permute-start.1) | collective-permute-done | bytes 2064416 | tf_op jit(solution)/shard_map/ppermute | solution.py:98
  379.4 3.1 fusion.20
  385.5 3.2 fusion.11
  391.5 3.2 collective-permute-start.5
  399.5 9.0 %collective-permute-done.6 = bf16[36,1536]{1,0:T(8,128)(2,1)S(1)} collective-permute-done((bf16[36,1536]{1,0:T(8,128)(2,1)}, bf16[36,1536]{1,0:T(8,128)(2,1)S(1)}, u32[]{:S(2)}, u32[]{:S(2)}) %collective-permute-start.6) | collective-permute-done | bytes 110624 | tf_op jit(solution)/shard_map/ppermute | solution.py:14
  410.0 6.1 %concatenate.15 = bf16[288,1536]{1,0:T(8,128)(2,1)S(1)} concatenate(bf16[36,1536]{1,0:T(8,128)(2,1)} %copy-done.15, bf16[36,1536]{1,0:T(8,128)(2,1)} %copy-done.14, bf16[36,1536]{1,0:T(8,128)(2,1)} %copy-done.13, bf16[36,1536]{1,0:T(8,128)(2,1)} %copy-done.12, bf16[36,1536]{1,0:T(8,128)(2,1)} %copy-done.11, bf16[36,1536]{1,0:T(8,128)(2,1)} %collective-permute-done.7, ...), dimensions={0} | concatenate | bytes 1769472 | tf_op jit(solution)/shard_map/concatenate | solution.py:15
  421.0 3.4 multiply_reduce_fusion
  424.4 8.3 %all-reduce.1 = (f32[2,12,12]{2,1,0:T(8,128)S(1)}, f32[2,12,12]{2,1,0:T(8,128)S(1)}) all-reduce(f32[2,12,12]{2,1,0:T(8,128)S(1)} %get-tuple-element.6, f32[2,12,12]{2,1,0:T(8,128)S(1)} %reduce_sum.529), channel_id=1, replica_groups=mesh['outer'=2,'sec'=8,'tp'=2] {'tp'}, use_global_device_ids=true, to_apply=%region_12.14 | all-reduce | flops 576 | bytes 4608 | tf_op jit(solution)/shard_map/psum | solution.py:118
  432.7 9.8 %multiply_reduce_fusion.1 = (f32[1536]{0:T(1024)S(1)}, f32[1536]{0:T(1024)S(1)}, f32[1536]{0:T(1024)S(1)}, f32[1536]{0:T(1024)S(1)}, f32[1536]{0:T(1024)S(1)}, /...) fusion(f32[2,12,12,1536]{3,2,1,0:T(8,128)S(1)} %convert_multipl, ...), kind=kLoop, calls=%fused_computation.93 | loop fusion | flops 19436544 | bytes 7200384 | tf_op jit(solution)/shard_map/reduce_sum | solution.py:128
  442.5 5.4 multiply_reduce_fusion.38
  448.0 6.3 %multiply_reduce_fusion.19 = (f32[1536]{0:T(1024)S(1)}, f32[1536]{0:T(1024)S(1)}, f32[1536]{0:T(1024)S(1)}, f32[1536]{0:T(1024)S(1)}, f32[1536]{0:T(1024)S(1)}, ...) fusion(f32[2,12,12,1536]{3,2,1,0:T(8,128)S(1)} %get-tuple-eleme, ...), kind=kLoop, calls=%fused_computation.111 | loop fusion | flops 15897600 | bytes 3649536 | tf_op jit(solution)/shard_map/reduce_sum | solution.py:128
  455.0 4.8 stack.207
  459.9 56.6 %all-reduce.7.cloned.1.call-done = f32[51,1536]{1,0:T(8,128)} async-done(((f32[51,1536]{1,0:T(8,128)}), f32[51,1536]{1,0:T(8,128)}) %all-reduce.7.cloned.1.call-update) | async-done | bytes 313360 | tf_op jit(solution)/shard_map/psum | solution.py:134
  518.2 5.5 psum.70
  526.2 5.5 fusion.2
  531.7 20.6 %all-reduce.9.cloned.1.call-done = f32[51,1536]{1,0:T(8,128)} async-done(((f32[51,1536]{1,0:T(8,128)}), f32[51,1536]{1,0:T(8,128)}) %all-reduce.9.cloned.1.call-update) | async-done | bytes 313360 | tf_op jit(solution)/shard_map/psum | solution.py:137
  (146 shorter events, 65.5 us)
Async XLA Ops:
  7.2 222.4 %all-gather.3.cloned.1.call-start = ((), (), s32[]{:S(2)}) async-start(), calls=%async_computation.3 | async-start | bytes 24772608 | tf_op jit(solution)/shard_map/all_gather | solution.py:69
  11.6 0.7 copy-start.16
  11.6 1.0 copy-start.4
  11.6 2.6 copy-start.1
  47.9 0.6 copy-start.5
  47.9 0.6 copy-start.7
  53.1 59.6 %all-to-all-start = ((bf16[8,36,1536]{2,1,0:T(8,128)(2,1)}), bf16[8,36,1536]{2,1,0:T(8,128)(2,1)S(1)}, u32[]{:S(2)}, u32[]{:S(2)}) async-start(bf16[8,36,1536]{2,1,0:T(8,128)(2,1)} %all_to_all.8), calls=%async_computation | async-start | bytes 1966080 | tf_op jit(solution)/shard_map/all_to_all | solution.py:73
  58.0 458.6 %all-reduce.7.cloned.1.call-start = ((), (), s32[]{:S(2)}) async-start(), calls=%async_computation.1 | async-start | bytes 688128 | tf_op jit(solution)/shard_map/psum | solution.py:134
  229.5 3.2 copy-start.3
  241.4 3.0 copy-start.17
  242.9 47.4 %collective-permute-start = (bf16[288,3584]{1,0:T(8,128)(2,1)}, bf16[288,3584]{1,0:T(8,128)(2,1)}, u32[]{:S(2)}, u32[]{:S(2)}) collective-permute-start(bf16[288,3584]{1,0:T(8,128)(2,1)} %pad_maximum_fusion), channel_id=1, source_target_pairs={{0,1},{1,0},{2,3},{3,2},{4,5},{5,4},{6,7},{7,6},{8,9},{9,8},{10,11... | collective-permute-start | bytes 6193160 | tf_op jit(solution)/shard_map/ppermute | solution.py:85
  293.7 9.7 %copy-start.9 = (f32[3584]{0:T(1024)S(1)}, f32[3584]{0:T(1024)}, u32[]{:S(2)}) copy-start(f32[3584]{0:T(1024)} %param.20) | copy-start | bytes 43012
  330.8 45.5 %collective-permute-start.1 = (bf16[288,3584]{1,0:T(8,128)(2,1)}, bf16[288,3584]{1,0:T(8,128)(2,1)}, u32[]{:S(2)}, u32[]{:S(2)}) collective-permute-start(bf16[288,3584]{1,0:T(8,128)(2,1)} %gather_fusion), channel_id=1, source_target_pairs={{0,1},{1,0},{2,3},{3,2},{4,5},{5,4},{6,7},{7,6},{8,9},{9,8},{10,11... | collective-permute-start | bytes 6193160 | tf_op jit(solution)/shard_map/ppermute | solution.py:98
  332.4 3.2 copy-start
  389.7 26.3 %copy-start.10 = (f32[1536]{0:T(1024)S(1)}, f32[1536]{0:T(1024)}, u32[]{:S(2)}) copy-start(f32[1536]{0:T(1024)} %param.15) | copy-start | bytes 18436
  390.6 7.0 %collective-permute-start.8 = (bf16[36,1536]{1,0:T(8,128)(2,1)S(1)}, bf16[36,1536]{1,0:T(8,128)(2,1)S(1)}, u32[]{:S(2)}, u32[]{:S(2)}) collective-permute-start(bf16[36,1536]{1,0:T(8,128)(2,1)S(1)} %get-tuple-element.125), channel_id=1, source_target_pairs={{0,2},{2,4},{4,6},{6,8},{8,10},{10,12},{12,14},{14,0},{1,3},{3,5},... | collective-permute-start | bytes 331784 | tf_op jit(solution)/shard_map/ppermute | solution.py:14
  390.6 8.2 %collective-permute-start.7 = (bf16[36,1536]{1,0:T(8,128)(2,1)S(1)}, bf16[36,1536]{1,0:T(8,128)(2,1)}, u32[]{:S(2)}, u32[]{:S(2)}) collective-permute-start(bf16[36,1536]{1,0:T(8,128)(2,1)S(1)} %get-tuple-element.126), channel_id=1, source_target_pairs={{0,4},{2,6},{4,8},{6,10},{8,12},{10,14},{12,0},{14,2},{1,5},{3,7},... | collective-permute-start | bytes 331784 | tf_op jit(solution)/shard_map/ppermute | solution.py:14
  390.6 17.9 %collective-permute-start.6 = (bf16[36,1536]{1,0:T(8,128)(2,1)}, bf16[36,1536]{1,0:T(8,128)(2,1)S(1)}, u32[]{:S(2)}, u32[]{:S(2)}) collective-permute-start(bf16[36,1536]{1,0:T(8,128)(2,1)} %get-tuple-element.127), channel_id=1, source_target_pairs={{0,6},{2,8},{4,10},{6,12},{8,14},{10,0},{12,2},{14,4},{1,7},{3,9},... | collective-permute-start | bytes 331784 | tf_op jit(solution)/shard_map/ppermute | solution.py:14
  391.5 17.1 %collective-permute-start.5 = (bf16[36,1536]{1,0:T(8,128)(2,1)}, bf16[36,1536]{1,0:T(8,128)(2,1)S(1)}, u32[]{:S(2)}, u32[]{:S(2)}) collective-permute-start(bf16[36,1536]{1,0:T(8,128)(2,1)} %get-tuple-element.128), channel_id=1, source_target_pairs={{0,8},{2,10},{4,12},{6,14},{8,0},{10,2},{12,4},{14,6},{1,9},{3,11}... | collective-permute-start | bytes 331784 | tf_op jit(solution)/shard_map/ppermute | solution.py:14
  394.7 13.9 %collective-permute-start.4 = (bf16[36,1536]{1,0:T(8,128)(2,1)}, bf16[36,1536]{1,0:T(8,128)(2,1)S(1)}, u32[]{:S(2)}, u32[]{:S(2)}) collective-permute-start(bf16[36,1536]{1,0:T(8,128)(2,1)} %get-tuple-element.129), channel_id=1, source_target_pairs={{0,10},{2,12},{4,14},{6,0},{8,2},{10,4},{12,6},{14,8},{1,11},{3,13... | collective-permute-start | bytes 331784 | tf_op jit(solution)/shard_map/ppermute | solution.py:14
  397.5 11.1 %collective-permute-start.3 = (bf16[36,1536]{1,0:T(8,128)(2,1)S(1)}, bf16[36,1536]{1,0:T(8,128)(2,1)S(1)}, u32[]{:S(2)}, u32[]{:S(2)}) collective-permute-start(bf16[36,1536]{1,0:T(8,128)(2,1)S(1)} %get-tuple-element.130), channel_id=1, source_target_pairs={{0,12},{2,14},{4,0},{6,2},{8,4},{10,6},{12,8},{14,10},{1,13},{3,15... | collective-permute-start | bytes 331784 | tf_op jit(solution)/shard_map/ppermute | solution.py:14
  398.8 9.8 %collective-permute-start.2 = (bf16[36,1536]{1,0:T(8,128)(2,1)S(1)}, bf16[36,1536]{1,0:T(8,128)(2,1)S(1)}, u32[]{:S(2)}, u32[]{:S(2)}) collective-permute-start(bf16[36,1536]{1,0:T(8,128)(2,1)S(1)} %get-tuple-element.131), channel_id=1, source_target_pairs={{0,14},{2,0},{4,2},{6,4},{8,6},{10,8},{12,10},{14,12},{1,15},{3,1}... | collective-permute-start | bytes 331784 | tf_op jit(solution)/shard_map/ppermute | solution.py:14
  408.5 0.6 copy-start.11
  408.6 0.7 copy-start.12
  408.6 0.7 copy-start.13
  408.6 0.7 copy-start.14
  409.3 0.6 copy-start.15
  418.1 2.9 copy-start.6
  418.1 2.9 copy-start.8
  432.7 9.8 %copy-start.2 = (bf16[2,12,12,1536]{3,0,2,1:T(2,128)(2,1)S(1)}, bf16[2,12,12,1536]{3,0,2,1:T(2,128)(2,1)}, u32[]{:S(2)}) copy-start(bf16[2,12,12,1536]{3,0,2,1:T(2,128)(2,1)} %param.12) | copy-start | bytes 2654212
  459.9 92.5 %all-reduce.9.cloned.1.call-start = ((), (), s32[]{:S(2)}) async-start(), calls=%async_computation.2 | async-start | bytes 688128 | tf_op jit(solution)/shard_map/psum | solution.py:137
Sparse Core Ops, SparseCore 0:
  11.8 217.7 all-gather.2
  460.0 56.5 all-reduce.6
  526.3 25.9 all-reduce.8
